TPU v7x, 32 devices: a whole 2x2x4 slice. The times are simulated.
32 devices in a mesh: row: 4 (over y, core), col: 8 (over z, x).
Axes of the slice: x: 2, y: 2, z: 4, core: 2. Of those that a mesh axis runs over, the one named last changes fastest.
Arguments:
- chol_window: bfloat16 [48, 48, 1536], P(None, None, ('row', 'col')), may hold values from -0.3125 to 0.3125
- chol_pairs: bfloat16 [512, 512, 1536], P('row', 'col'), may hold values from -0.3125 to 0.3125
- amplitudes: bfloat16 [48, 512, 1024], P(None, 'col', 'row'), may hold values from -6 to 6
- eps_window: float32 [48], P('col'), may hold values from 0.5 to 2
- eps_virtual: float32 [512], P('row'), may hold values from 0.5 to 2
- eps_occupied: float32 [1024], replicated, may hold values from 0.5 to 2
- dress_first: bfloat16 [1024, 1024], replicated, may hold values from -0.1875 to 0.1875
- dress_second: bfloat16 [1024, 1024], replicated, may hold values from -0.1875 to 0.1875
Outputs:
- resid: bfloat16 [48, 512, 1024], P('col', None, 'row')
All inputs are finite; a program needn't handle non-finite values.
Results may differ from a plain program's by a relative error of at most 0.0061.
Values may be sent and summed in bfloat16 or wider, within the bound.
A program may use at most 192 MiB of HBM per device.

v0:
```python
import jax
import jax.numpy as jnp
from jax import lax
from jax.sharding import PartitionSpec as P


def local(
    chol_window,
    chol_pairs,
    amplitudes,
    eps_window,
    eps_virtual,
    eps_occupied,
    dress_first,
    dress_second,
):
    window = lax.all_gather(chol_window, ("row", "col"), axis=2, tiled=True)
    block_b, block_d, aux_count = chol_pairs.shape
    window_size = window.shape[0]
    groups = window_size // 8
    window_blocks = window.reshape(groups, 8, window_size, aux_count)

    def build_tile(block_index):
        slab = lax.dynamic_index_in_dim(window_blocks, block_index, 0, keepdims=False)
        values = jnp.einsum("acq,bdq->abcd", slab, chol_pairs, preferred_element_type=jnp.float32)
        return values.astype(jnp.bfloat16)

    integrals = lax.map(build_tile, jnp.arange(groups, dtype=jnp.int32))
    integrals = integrals.reshape(window_size, block_b, window_size, block_d)
    partial_value = jnp.einsum(
        "abcd,cdo->abo",
        integrals,
        lax.all_gather(amplitudes, "row", axis=2, tiled=True),
        preferred_element_type=jnp.float32,
    )
    summed = lax.psum_scatter(partial_value, "col", scatter_dimension=0, tiled=True)
    rows_a = summed.shape[0]
    occ_count = summed.shape[2]
    denominator = (
        eps_window[:, None, None] + eps_virtual[None, :, None] + eps_occupied[None, None, :]
    )
    scaled = (summed / denominator).astype(jnp.bfloat16)
    flattened = scaled.reshape(rows_a * block_b, occ_count)
    first_mix = jnp.dot(flattened, dress_first, preferred_element_type=jnp.float32).astype(
        jnp.bfloat16
    )
    mixed = flattened.astype(jnp.float32) + jnp.dot(
        first_mix, dress_second, preferred_element_type=jnp.float32
    )
    mixed = mixed.astype(jnp.bfloat16).reshape(rows_a, block_b, occ_count)
    return lax.all_to_all(mixed, "row", split_axis=2, concat_axis=1, tiled=True)


def solution(mesh):
    return jax.shard_map(
        local,
        mesh=mesh,
        in_specs=(
            P(None, None, ("row", "col")),
            P("row", "col", None),
            P(None, "col", "row"),
            P("col"),
            P("row"),
            P(),
            P(),
            P(),
        ),
        out_specs=P("col", None, "row"),
        check_vma=False,
    )
```

profile of v0, /device:TPU:0, one launch (start us, length us, event | category | flops | bytes accessed | tf_op | source)
XLA Modules:
  0.0 796.6 jit_solution(15824649646967900453)
XLA Ops:
  6.5 2.5 copy.12
  9.0 0.0 all-gather.3.cloned.1.call-update
  9.0 0.0 all-gather.5.cloned.1.call-start
  9.1 0.7 all-gather.5.cloned.1.call-update
  9.8 0.0 reduce-scatter.2.cloned.1.call-start
  9.8 27.0 %copy.14 = bf16[128,64,1536]{2,0,1:T(8,128)(2,1)} copy(bf16[128,64,1536]{2,1,0:T(8,128)(2,1)} %param.11) | data formatting | bytes 50331648 | tf_op jit(solution)/shard_map/while | solution.py:28
  36.9 100.9 %all-gather.3.cloned.1.call-done = bf16[48,48,1536]{1,0,2:T(8,128)(2,1)} async-done(((bf16[48,48,48]{1,0,2:T(8,128)(2,1)}), bf16[48,48,1536]{1,0,2:T(8,128)(2,1)}) %all-gather.3.cloned.1.call-update) | async-done | bytes 7077904 | tf_op jit(solution)/shard_map/all_gather | solution.py:17
  137.8 20.5 %copy.13 = bf16[6,8,48,1536]{3,2,1,0:T(8,128)(2,1)} copy(bf16[6,8,48,1536]{2,1,0,3:T(8,128)(2,1)} %bitcast.40) | data formatting | bytes 14155776 | tf_op jit(solution)/shard_map/while | solution.py:28
  158.2 109.6 %while.10 = (s32[]{:T(128)}, bf16[6,8,128,48,64]{2,3,4,1,0:T(8,128)(2,1)}, s32[6]{0:T(128)S(1)}, bf16[6,8,48,1536]{3,2,1,0:T(8,128)(2,1)}, bf16[128,64,1536]{2,0...) while((s32[]{:T(128)}, bf16[6,8,128,48,64]{2,3,4,1,0:T(8,128)(2,1)}, s32[6]{0:T(128)S(1)}, ...), condition=%wide.region_1.2_spmd, body=%wide.region_0.1_spmd.sunk | while | flops 9666822144 | bytes 32637576 | solution.py:28
  158.2 0.6 dynamic_slice.15
  160.8 15.8 %bitcast_dynamic-update-slice_fusion.2 = bf16[6,8,128,48,64]{2,3,4,1,0:T(8,128)(2,1)} fusion(bf16[6,8,128,48,64]{2,3,4,1,0:T(8,128)(2,1)} %get-tuple-element.93, s32[]{:T(128)} %get-tuple-element.92, bf16[128,64,1536]{2,0,1:T(8,128)(2,1)} %get-tuple-element.104, bf16[6,8,48,1536]{3,2,1,0:T(8,128)(2,1)} %get-tuple-element.103, s32[]{:T(128)S(6)} %select_n.5), kind=kOutput, calls=%fused_computation.2.clone.1 | convolution fusion | flops 9666822144 | bytes 32637444 | tf_op jit(solution)/shard_map/while/body/eval_jaxpr/acq,bdq->abcd/dot_general | solution.py:25
  176.5 0.6 dynamic_slice.15
  179.1 15.8 %bitcast_dynamic-update-slice_fusion.2 = bf16[6,8,128,48,64]{2,3,4,1,0:T(8,128)(2,1)} fusion(bf16[6,8,128,48,64]{2,3,4,1,0:T(8,128)(2,1)} %get-tuple-element.93, s32[]{:T(128)} %get-tuple-element.92, bf16[128,64,1536]{2,0,1:T(8,128)(2,1)} %get-tuple-element.104, bf16[6,8,48,1536]{3,2,1,0:T(8,128)(2,1)} %get-tuple-element.103, s32[]{:T(128)S(6)} %select_n.5), kind=kOutput, calls=%fused_computation.2.clone.1 | convolution fusion | flops 9666822144 | bytes 32637444 | tf_op jit(solution)/shard_map/while/body/eval_jaxpr/acq,bdq->abcd/dot_general | solution.py:25
  194.8 0.6 dynamic_slice.15
  197.3 15.8 %bitcast_dynamic-update-slice_fusion.2 = bf16[6,8,128,48,64]{2,3,4,1,0:T(8,128)(2,1)} fusion(bf16[6,8,128,48,64]{2,3,4,1,0:T(8,128)(2,1)} %get-tuple-element.93, s32[]{:T(128)} %get-tuple-element.92, bf16[128,64,1536]{2,0,1:T(8,128)(2,1)} %get-tuple-element.104, bf16[6,8,48,1536]{3,2,1,0:T(8,128)(2,1)} %get-tuple-element.103, s32[]{:T(128)S(6)} %select_n.5), kind=kOutput, calls=%fused_computation.2.clone.1 | convolution fusion | flops 9666822144 | bytes 32637444 | tf_op jit(solution)/shard_map/while/body/eval_jaxpr/acq,bdq->abcd/dot_general | solution.py:25
  213.1 0.6 dynamic_slice.15
  215.6 15.7 %bitcast_dynamic-update-slice_fusion.2 = bf16[6,8,128,48,64]{2,3,4,1,0:T(8,128)(2,1)} fusion(bf16[6,8,128,48,64]{2,3,4,1,0:T(8,128)(2,1)} %get-tuple-element.93, s32[]{:T(128)} %get-tuple-element.92, bf16[128,64,1536]{2,0,1:T(8,128)(2,1)} %get-tuple-element.104, bf16[6,8,48,1536]{3,2,1,0:T(8,128)(2,1)} %get-tuple-element.103, s32[]{:T(128)S(6)} %select_n.5), kind=kOutput, calls=%fused_computation.2.clone.1 | convolution fusion | flops 9666822144 | bytes 32637444 | tf_op jit(solution)/shard_map/while/body/eval_jaxpr/acq,bdq->abcd/dot_general | solution.py:25
  231.3 0.6 dynamic_slice.15
  233.8 15.7 %bitcast_dynamic-update-slice_fusion.2 = bf16[6,8,128,48,64]{2,3,4,1,0:T(8,128)(2,1)} fusion(bf16[6,8,128,48,64]{2,3,4,1,0:T(8,128)(2,1)} %get-tuple-element.93, s32[]{:T(128)} %get-tuple-element.92, bf16[128,64,1536]{2,0,1:T(8,128)(2,1)} %get-tuple-element.104, bf16[6,8,48,1536]{3,2,1,0:T(8,128)(2,1)} %get-tuple-element.103, s32[]{:T(128)S(6)} %select_n.5), kind=kOutput, calls=%fused_computation.2.clone.1 | convolution fusion | flops 9666822144 | bytes 32637444 | tf_op jit(solution)/shard_map/while/body/eval_jaxpr/acq,bdq->abcd/dot_general | solution.py:25
  249.6 0.6 dynamic_slice.15
  252.1 15.8 %bitcast_dynamic-update-slice_fusion.2 = bf16[6,8,128,48,64]{2,3,4,1,0:T(8,128)(2,1)} fusion(bf16[6,8,128,48,64]{2,3,4,1,0:T(8,128)(2,1)} %get-tuple-element.93, s32[]{:T(128)} %get-tuple-element.92, bf16[128,64,1536]{2,0,1:T(8,128)(2,1)} %get-tuple-element.104, bf16[6,8,48,1536]{3,2,1,0:T(8,128)(2,1)} %get-tuple-element.103, s32[]{:T(128)S(6)} %select_n.5), kind=kOutput, calls=%fused_computation.2.clone.1 | convolution fusion | flops 9666822144 | bytes 32637444 | tf_op jit(solution)/shard_map/while/body/eval_jaxpr/acq,bdq->abcd/dot_general | solution.py:25
  267.8 71.1 %convolution_bitcast_fusion = f32[48,128,1024]{2,1,0:T(8,128)} fusion(bf16[48,128,48,64]{1,2,3,0:T(8,128)(2,1)} %bitcast.45, bf16[48,64,1024,1]{2,1,0,3:T(8,128)(2,1)} %bitcast.44), kind=kOutput, calls=%fused_computation.6 | convolution fusion | flops 38654705664 | bytes 69206016 | tf_op jit(solution)/shard_map/abcd,cdo->abo/dot_general | solution.py:30
  338.9 0.0 reduce-scatter.2.cloned.1.call-update
  339.0 0.6 copy-done.2
  339.6 0.0 copy-done.3
  339.6 0.1 broadcast_add_fusion
  339.7 401.4 %reduce-scatter.2.cloned.1.call-done = f32[6,128,1024]{2,1,0:T(8,128)} async-done(((f32[48,128,1024]{2,1,0:T(8,128)}), f32[6,128,1024]{2,1,0:T(8,128)}) %reduce-scatter.2.cloned.1.call-update) | async-done | bytes 3145744 | tf_op jit(solution)/shard_map/reduce_scatter | solution.py:36
  741.1 3.5 divide_convert_fusion
  744.6 7.2 add_convert_fusion
  751.8 4.0 copy.16
  755.8 30.1 %all_to_all.18 = bf16[6,128,1024]{1,0,2:T(8,128)(2,1)} all-to-all(bf16[6,128,1024]{1,0,2:T(8,128)(2,1)} %copy.16), channel_id=1, replica_groups=mesh['row'=4,'col'=8] {'row'}, dimensions={2} | all-to-all | bytes 3145728 | tf_op jit(solution)/shard_map/all_to_all | solution.py:51
  785.9 4.1 copy.17
  (10 shorter events, 0.0 us)
Async XLA Ops:
  6.5 738.1 %copy-start = (bf16[1024,1024]{1,0:T(8,128)(2,1)S(1)}, bf16[1024,1024]{1,0:T(8,128)(2,1)}, u32[]{:S(2)}) copy-start(bf16[1024,1024]{1,0:T(8,128)(2,1)} %param.17) | copy-start | bytes 6291460
  6.5 131.2 %all-gather.3.cloned.1.call-start = ((), (), s32[]{:S(2)}) async-start(), calls=%async_computation.2 | async-start | bytes 19464192 | tf_op jit(solution)/shard_map/all_gather | solution.py:17
  9.0 258.8 %all-gather.5.cloned.1.call-start = ((), (), s32[]{:S(2)}) async-start(), calls=%async_computation.3 | async-start | bytes 7864320 | tf_op jit(solution)/shard_map/all_gather | solution.py:33
  9.8 731.3 %reduce-scatter.2.cloned.1.call-start = ((), (), s32[]{:S(2)}) async-start(), calls=%async_computation.4 | async-start | bytes 28311552 | tf_op jit(solution)/shard_map/reduce_scatter | solution.py:36
  338.9 0.7 copy-start.2
  338.9 0.7 copy-start.3
  338.9 402.1 %copy-start.1 = (f32[1024]{0:T(1024)S(1)}, f32[1024]{0:T(1024)}, u32[]{:S(2)}) copy-start(f32[1024]{0:T(1024)} %param.15) | copy-start | bytes 12292
Sparse Core Ops, SparseCore 0:
  10.3 127.3 all-gather.2
  139.3 45.3 all-gather.4
  339.1 401.9 reduce-scatter.1
where the time goes:
time: 798 us; the launch traced here: 797 us
  waiting for transfers between devices  503 us (63%)
  matrix products  173 us (22%)
  local copies, waits for them, and re-layouts  62.3 us (8%)
  blocking collectives  30.1 us (4%)
  between operations  13.1 us (2%)
  loops' own time  11.7 us (1%)
    reduce_scatter x1, waiting for transfers between devices, local(): lax.psum_scatter(partial_value, 'col', scatter_dimension=0, tiled=True)  401 us
    all_gather x1, waiting for transfers between devices, local(): window = lax.all_gather(chol_window, ('row', 'col'), axis=2, tiled=True)  101 us
    dot_general x6, matrix products, build_tile(): jnp.einsum('acq,bdq->abcd', slab, chol_pairs, preferred_element_type=jnp....  94.4 us
    dot_general x1, matrix products, local(): jnp.einsum('abcd,cdo->abo', integrals, lax.all_gather(amplitudes, 'row',...  71.1 us
    while x2, local copies, waits for them, and re-layouts, local(): integrals = lax.map(build_tile, jnp.arange(groups, dtype=jnp.int32))  47.5 us
    all_to_all x1, blocking collectives, local(): return lax.all_to_all(mixed, 'row', split_axis=2, concat_axis=1, tiled=True)  30.1 us
  transfers between devices with their start and end apart: 3, of which 2 were waited for; matrix products, arithmetic and copies ran while one was open for 18% of the time, Pallas kernels for 0%

commit v1 on v0

v1 whole, which is shorter than its diff:
```python
import functools

import jax
import jax.numpy as jnp
from jax import lax
from jax.experimental import pallas as pl
from jax.experimental.pallas import tpu as pltpu
from jax.sharding import PartitionSpec as P

F32 = jnp.float32
BF16 = jnp.bfloat16


def ladder_kernel(rows, win, block_b, window_ref, pairs_ref, amps_ref, out_ref, mixed):
    step = pl.program_id(0)
    count = pairs_ref.shape[0] // block_b
    pair = 2 if count % 2 == 0 else 1

    def body(index, carry):
        start = pl.multiple_of(index * (pair * block_b), pair * block_b)
        tile = pairs_ref[pl.ds(start, pair * block_b), :]
        values = lax.dot_general(
            window_ref[...], tile, (((1,), (1,)), ((), ())), preferred_element_type=F32
        ).astype(BF16)
        for k in range(pair):
            at = pl.multiple_of((step * count + index * pair + k) * win, win)
            for a in range(rows):
                mixed[pl.ds(at, win), a * block_b : (a + 1) * block_b] = values[
                    a * win : (a + 1) * win, k * block_b : (k + 1) * block_b
                ]
        return carry

    lax.fori_loop(0, count // pair, body, 0)

    @pl.when(step == pl.num_programs(0) - 1)
    def _():
        width = 256

        def contract(index, carry):
            at = pl.multiple_of(index * width, width)
            out_ref[:, pl.ds(at, width)] = jnp.dot(
                amps_ref[...], mixed[:, pl.ds(at, width)], preferred_element_type=F32
            ).astype(BF16)
            return carry

        lax.fori_loop(0, out_ref.shape[1] // width, contract, 0)


def ladder_part(window, pairs, amps, rows, block_b):
    win = window.shape[0] // rows
    depth = pairs.shape[1]
    block_d = pairs.shape[0] // block_b
    occ = amps.shape[0]
    if block_b % 128 or win % 16 or (rows * block_b) % 256 or block_d % 8:
        values = jnp.einsum(
            "acq,dbq->dcab",
            window.reshape(rows, win, depth),
            pairs.reshape(block_d, block_b, depth),
            preferred_element_type=F32,
        ).astype(BF16)
        values = values.reshape(block_d * win, rows * block_b)
        return jnp.dot(amps, values, preferred_element_type=F32).astype(BF16)
    group = 8 * block_b
    total = block_d * win
    return pl.pallas_call(
        functools.partial(ladder_kernel, rows, win, block_b),
        out_shape=jax.ShapeDtypeStruct((occ, rows * block_b), BF16),
        grid=(pairs.shape[0] // group,),
        in_specs=[
            pl.BlockSpec(window.shape, lambda i: (0, 0)),
            pl.BlockSpec((group, depth), lambda i: (i, 0)),
            pl.BlockSpec(amps.shape, lambda i: (0, 0)),
        ],
        out_specs=pl.BlockSpec((occ, rows * block_b), lambda i: (0, 0)),
        scratch_shapes=[pltpu.VMEM((total, rows * block_b), BF16)],
        compiler_params=pltpu.CompilerParams(
            dimension_semantics=("arbitrary",), vmem_limit_bytes=48 * 1024 * 1024
        ),
        cost_estimate=pl.CostEstimate(
            flops=2 * rows * block_b * total * (depth + occ),
            bytes_accessed=2 * (pairs.size + amps.size + window.size + occ * rows * block_b),
            transcendentals=0,
        ),
    )(window, pairs, amps)


def add(left, right):
    return left.astype(F32) + right.astype(F32)


def local(
    cols,
    chol_window,
    chol_pairs,
    amplitudes,
    eps_window,
    eps_virtual,
    eps_occupied,
    dress_first,
    dress_second,
):
    win = chol_window.shape[0]
    block_b, block_d, depth = chol_pairs.shape
    rows = win // cols
    occ = eps_occupied.shape[0]

    inner = 1 << ((cols.bit_length() - 1) // 2)
    outer = cols // inner
    me = lax.axis_index("col")
    my_outer, my_inner = me // inner, lax.rem(me, inner)
    next_inner = [(o * inner + i, o * inner + (i + 1) % inner) for o in range(outer) for i in range(inner)]
    next_outer = [(o * inner + i, ((o + 1) % outer) * inner + i) for o in range(outer) for i in range(inner)]

    window = chol_window.reshape(win * win, -1).T
    window = lax.all_gather(window, "col", axis=0, tiled=True)
    window = lax.all_gather(window, "row", axis=0, tiled=True)
    window = window.T
    amps = amplitudes.transpose(2, 1, 0).reshape(amplitudes.shape[2], block_d * win)
    amps = lax.all_gather(amps, "row", axis=0, tiled=True)
    pairs = chol_pairs.transpose(1, 0, 2).reshape(block_d * block_b, depth)

    def part(to_outer, to_inner):
        target = to_outer * inner + to_inner
        piece = lax.dynamic_slice_in_dim(window, target * (rows * win), rows * win, 0)
        return ladder_part(piece, pairs, amps, rows, block_b)

    moving = None
    for hop in range(outer):
        to_outer = lax.rem(my_outer + (2 * outer - 1 - hop), outer)
        held = None
        for step in range(inner):
            to_inner = lax.rem(my_inner + (2 * inner - 1 - step), inner)
            mine = part(to_outer, to_inner)
            held = mine if held is None else add(held, mine)
            if step < inner - 1:
                held = lax.ppermute(held.astype(BF16), "col", next_inner)
        held = held if moving is None else add(moving, held)
        if hop < outer - 1:
            moving = lax.ppermute(held.astype(BF16), "col", next_outer)

    summed = held.T.reshape(rows, block_b, occ)
    denominator = (
        eps_window[:, None, None] + eps_virtual[None, :, None] + eps_occupied[None, None, :]
    )
    scaled = (summed / denominator).astype(BF16)
    flattened = scaled.reshape(rows * block_b, occ)
    first_mix = jnp.dot(flattened, dress_first, preferred_element_type=F32).astype(BF16)
    mixed = flattened.astype(F32) + jnp.dot(first_mix, dress_second, preferred_element_type=F32)
    mixed = mixed.astype(BF16).reshape(rows, block_b, occ)
    return lax.all_to_all(mixed, "row", split_axis=2, concat_axis=1, tiled=True)


def solution(mesh):
    return jax.shard_map(
        functools.partial(local, mesh.shape["col"]),
        mesh=mesh,
        in_specs=(
            P(None, None, ("row", "col")),
            P("row", "col", None),
            P(None, "col", "row"),
            P("col"),
            P("row"),
            P(),
            P(),
            P(),
        ),
        out_specs=P("col", None, "row"),
        check_vma=False,
    )
```

time: 798 us -> 433 us (0.54)
  waiting for transfers between devices: 503 us -> 117 us
  Pallas kernels: 0 us -> 190 us
  matrix products: 173 us -> 9.82 us
  loops' own time: 11.7 us -> 0 us
  starting transfers between devices: 0.08 us -> 9.46 us
    reduce_scatter x1 -> x0, waiting for transfers between devices: 401 us -> none  [local(): lax.psum_scatter(partial_value, 'col', scatter_dimension=0, tiled=True)]
    pallas_call x0 -> x8, Pallas kernels: none -> 190 us  [ladder_part(): pl.pallas_call(functools.partial(ladder_kernel, rows, win, block_b), out_...]
    dot_general x8 -> x1, matrix products: 173 us -> 9.82 us  [local(): jnp.dot(first_mix, dress_second, preferred_element_type=F32)]
    while x2 -> x0, local copies, waits for them, and re-layouts: 47.5 us -> none  [local(): integrals = lax.map(build_tile, jnp.arange(groups, dtype=jnp.int32))]
    transpose x0 -> x1, local copies, waits for them, and re-layouts: none -> 27.3 us  [local(): pairs = chol_pairs.transpose(1, 0, 2).reshape(block_d * block_b, depth)]
    another operation x1 -> x0, loops' own time: 11.7 us -> none  [local(): integrals = lax.map(build_tile, jnp.arange(groups, dtype=jnp.int32))]
    ppermute x0 -> x7, starting transfers between devices: none -> 9.37 us  [the longest x3 5.04 us: local(): moving = lax.ppermute(held.astype(BF16), 'col', next_outer)]
    ppermute x0 -> x7, waiting for transfers between devices: none -> 9.09 us  [the longest x3 9.08 us: local(): moving = lax.ppermute(held.astype(BF16), 'col', next_outer)]
  transfers between devices with their start and end apart: 3 -> 10, of which waited for: 2 -> 4; matrix products, arithmetic and copies ran while one was open for 18% -> 9% of each run, Pallas kernels for 0% -> 39%
where the time goes in v1:
time: 433 us; the launch traced here: 431 us
  Pallas kernels  190 us (44%)
  waiting for transfers between devices  117 us (27%)
  local copies, waits for them, and re-layouts  59.3 us (14%)
  blocking collectives  30.2 us (7%)
  between operations  13.4 us (3%)
  matrix products  9.82 us (2%)
  starting transfers between devices  9.46 us (2%)
    pallas_call x8, Pallas kernels, ladder_part(): pl.pallas_call(functools.partial(ladder_kernel, rows, win, block_b), out_...  190 us
    all_gather x1, waiting for transfers between devices, local(): window = lax.all_gather(window, 'col', axis=0, tiled=True)  49.5 us
    all_gather x1, waiting for transfers between devices, local(): amps = lax.all_gather(amps, 'row', axis=0, tiled=True)  42.3 us
    all_to_all x1, blocking collectives, local(): return lax.all_to_all(mixed, 'row', split_axis=2, concat_axis=1, tiled=True)  30.2 us
    transpose x1, local copies, waits for them, and re-layouts, local(): pairs = chol_pairs.transpose(1, 0, 2).reshape(block_d * block_b, depth)  27.3 us
    all_gather x1, waiting for transfers between devices, local(): window = lax.all_gather(window, 'row', axis=0, tiled=True)  16.4 us
    dot_general x1, matrix products, local(): jnp.dot(first_mix, dress_second, preferred_element_type=F32)  9.82 us
    ppermute x3, waiting for transfers between devices, local(): moving = lax.ppermute(held.astype(BF16), 'col', next_outer)  9.08 us
  transfers between devices with their start and end apart: 10, of which 4 were waited for; matrix products, arithmetic and copies ran while one was open for 9% of the time, Pallas kernels for 39%

profile of v1, /device:TPU:0, one launch (start us, length us, event | category | flops | bytes accessed | tf_op | source)
XLA Modules:
  0.0 430.7 jit_solution(615320582553183410)
XLA Ops:
  6.5 2.1 copy.29
  8.7 49.5 %all-gather.4.cloned.1.call-done = bf16[384,2304]{1,0:T(8,128)(2,1)} async-done(((bf16[48,2304]{1,0:T(8,128)(2,1)}), bf16[384,2304]{1,0:T(8,128)(2,1)}) %all-gather.4.cloned.1.call-update) | async-done | bytes 1769488 | tf_op jit(solution)/shard_map/all_gather | solution.py:115
  58.2 3.9 copy.20
  62.2 3.4 copy.22
  65.6 2.6 copy.23
  68.3 27.3 %copy.21 = bf16[64,128,1536]{2,1,0:T(8,128)(2,1)} copy(bf16[64,128,1536]{2,0,1:T(8,128)(2,1)} %bitcast.43) | data formatting | bytes 50331648 | tf_op jit(solution)/shard_map/transpose | solution.py:120
  95.6 16.4 %all-gather.6.cloned.1.call-done = bf16[1536,2304]{0,1:T(8,128)(2,1)} async-done(((bf16[384,2304]{0,1:T(8,128)(2,1)}), bf16[1536,2304]{0,1:T(8,128)(2,1)}) %all-gather.6.cloned.1.call-update) | async-done | bytes 7077904 | tf_op jit(solution)/shard_map/all_gather | solution.py:116
  112.0 5.7 %dynamic-slice_bitcast_fusion.7 = (bf16[288,1536]{1,0:T(8,128)(2,1)}, bf16[288,1536]{1,0:T(8,128)(2,1)S(1)}, bf16[288,1536]{1,0:T(8,128)(2,1)}, bf16[288,1536]{1...) fusion(bf16[1536,2304]{0,1:T(8,128)(2,1)} %all-gather.6.cloned., ...), kind=kLoop, calls=%fused_computation.14 | loop fusion | bytes 14155808 | tf_op jit(solution)/shard_map/dynamic_slice | solution.py:124
  117.8 42.3 %all-gather.8.cloned.1.call-done.amps_ref = bf16[1024,3072]{1,0:T(8,128)(2,1)} async-done(((bf16[256,3072]{1,0:T(8,128)(2,1)}), bf16[1024,3072]{1,0:T(8,128)(2,1)}) %all-gather.8.cloned.1.call-update) | async-done | bytes 6291472 | tf_op jit(solution)/shard_map/all_gather | solution.py:119
  160.0 1.2 copy-done.7
  161.2 23.7 %shard_map.82 = bf16[1024,768]{1,0:T(8,128)(2,1)S(1)} custom-call(bf16[288,1536]{1,0:T(8,128)(2,1)S(1)} %copy-done.7, bf16[8192,1536]{1,0:T(8,128)(2,1)} %bitcast.44, bf16[1024,3072]{1,0:T(8,128)(2,1)} %all-gather.8.cloned.1.call-done.amps_ref), custom_call_target="tpu_custom_call" | custom-call | flops 12079595520 | bytes 33914880 | tf_op jit(solution)/shard_map/pallas_call | solution.py:65
  184.9 1.5 collective-permute-start
  186.5 23.7 %shard_map.84 = bf16[1024,768]{1,0:T(8,128)(2,1)S(1)} custom-call(bf16[288,1536]{1,0:T(8,128)(2,1)S(1)} %copy-done.6, bf16[8192,1536]{1,0:T(8,128)(2,1)} %bitcast.45, bf16[1024,3072]{1,0:T(8,128)(2,1)} %all-gather.8.cloned.1.call-done.amps_ref), custom_call_target="tpu_custom_call" | custom-call | flops 12079595520 | bytes 33914880 | tf_op jit(solution)/shard_map/pallas_call | solution.py:65
  210.2 0.7 collective-permute-start.2
  210.9 23.7 %shard_map.83 = bf16[1024,768]{1,0:T(8,128)(2,1)S(1)} custom-call(bf16[288,1536]{1,0:T(8,128)(2,1)S(1)} %copy-done.5, bf16[8192,1536]{1,0:T(8,128)(2,1)} %bitcast.46, bf16[1024,3072]{1,0:T(8,128)(2,1)} %all-gather.8.cloned.1.call-done.amps_ref), custom_call_target="tpu_custom_call" | custom-call | flops 12079595520 | bytes 33914880 | tf_op jit(solution)/shard_map/pallas_call | solution.py:65
  235.0 1.7 collective-permute-start.1
  236.7 23.7 %shard_map.86 = bf16[1024,768]{1,0:T(8,128)(2,1)S(1)} custom-call(bf16[288,1536]{1,0:T(8,128)(2,1)S(1)} %copy-done.4, bf16[8192,1536]{1,0:T(8,128)(2,1)} %bitcast.47, bf16[1024,3072]{1,0:T(8,128)(2,1)} %all-gather.8.cloned.1.call-done.amps_ref), custom_call_target="tpu_custom_call" | custom-call | flops 12079595520 | bytes 33914880 | tf_op jit(solution)/shard_map/pallas_call | solution.py:65
  260.5 1.5 collective-permute-start.4
  262.0 23.7 %shard_map.85 = bf16[1024,768]{1,0:T(8,128)(2,1)S(1)} custom-call(bf16[288,1536]{1,0:T(8,128)(2,1)S(1)} %copy-done.3, bf16[8192,1536]{1,0:T(8,128)(2,1)} %bitcast.48, bf16[1024,3072]{1,0:T(8,128)(2,1)} %all-gather.8.cloned.1.call-done.amps_ref), custom_call_target="tpu_custom_call" | custom-call | flops 12079595520 | bytes 33914880 | tf_op jit(solution)/shard_map/pallas_call | solution.py:65
  286.2 1.6 collective-permute-start.3
  287.8 23.8 %shard_map.88 = bf16[1024,768]{1,0:T(8,128)(2,1)S(1)} custom-call(bf16[288,1536]{1,0:T(8,128)(2,1)S(1)} %copy-done.2, bf16[8192,1536]{1,0:T(8,128)(2,1)} %bitcast.49, bf16[1024,3072]{1,0:T(8,128)(2,1)} %all-gather.8.cloned.1.call-done.amps_ref), custom_call_target="tpu_custom_call" | custom-call | flops 12079595520 | bytes 33914880 | tf_op jit(solution)/shard_map/pallas_call | solution.py:65
  312.2 23.7 %shard_map.87 = bf16[1024,768]{1,0:T(8,128)(2,1)S(1)} custom-call(bf16[288,1536]{1,0:T(8,128)(2,1)S(1)} %copy-done.1, bf16[8192,1536]{1,0:T(8,128)(2,1)} %bitcast.50, bf16[1024,3072]{1,0:T(8,128)(2,1)} %all-gather.8.cloned.1.call-done.amps_ref), custom_call_target="tpu_custom_call" | custom-call | flops 12079595520 | bytes 33914880 | tf_op jit(solution)/shard_map/pallas_call | solution.py:65
  336.5 1.8 collective-permute-start.5
  338.4 23.7 %shard_map.89 = bf16[1024,768]{1,0:T(8,128)(2,1)S(1)} custom-call(bf16[288,1536]{1,0:T(8,128)(2,1)S(1)} %get-tuple-element.6.window_ref, bf16[8192,1536]{1,0:T(8,128)(2,1)} %bitcast.51, bf16[1024,3072]{1,0:T(8,128)(2,1)} %all-gather.8.cloned.1.call-done.amps_ref), custom_call_target="tpu_custom_call" | custom-call | flops 12079595520 | bytes 33914880 | tf_op jit(solution)/shard_map/pallas_call | solution.py:65
  362.1 1.1 copy-done.8
  363.2 1.2 copy-done.11
  364.4 9.1 %collective-permute-done.5 = bf16[1024,768]{1,0:T(8,128)(2,1)} collective-permute-done((bf16[1024,768]{1,0:T(8,128)(2,1)S(1)}, bf16[1024,768]{1,0:T(8,128)(2,1)}, u32[]{:S(2)}, u32[]{:S(2)}) %collective-permute-start.5) | collective-permute-done | bytes 1572896 | tf_op jit(solution)/shard_map/ppermute | solution.py:139
  373.5 9.8 %add_convert_fusion = bf16[768,1024]{0,1:T(8,128)(2,1)} fusion(bf16[1024,1024]{1,0:T(8,128)(2,1)S(1)} %copy-done, bf16[1024,1024]{1,0:T(8,128)(2,1)} %param.14, f32[1024]{0:T(1024)S(1)} %copy-done.12, f32[768]{0:T(1024)S(1)} %bitcast_add_fusion, bf16[1024,768]{1,0:T(8,128)(2,1)} %copy-done.8, bf16[1024,768]{1,0:T(8,128)(2,1)} %copy-done.11, ...), kind=kOutput, calls=%fused_computation.2 | convolution fusion | flops 3236954112 | bytes 10492928 | tf_op jit(solution)/shard_map/dot_general | solution.py:148
  383.3 2.6 copy.25
  385.9 4.0 copy.26
  389.9 30.2 %all_to_all.18 = bf16[6,128,1024]{1,0,2:T(8,128)(2,1)} all-to-all(bf16[6,128,1024]{1,0,2:T(8,128)(2,1)} %copy.26), channel_id=1, replica_groups=mesh['row'=4,'col'=8] {'row'}, dimensions={2} | all-to-all | bytes 3145728 | tf_op jit(solution)/shard_map/all_to_all | solution.py:150
  420.1 4.1 copy.27
  (41 shorter events, 2.4 us)
Async XLA Ops:
  6.5 367.0 %copy-start = (bf16[1024,1024]{1,0:T(8,128)(2,1)S(1)}, bf16[1024,1024]{1,0:T(8,128)(2,1)}, u32[]{:S(2)}) copy-start(bf16[1024,1024]{1,0:T(8,128)(2,1)} %param.15) | copy-start | bytes 6291460
  6.5 51.7 %all-gather.4.cloned.1.call-start = ((), (), s32[]{:S(2)}) async-start(), calls=%async_computation.1 | async-start | bytes 1990656 | tf_op jit(solution)/shard_map/all_gather | solution.py:115
  8.7 103.4 %all-gather.6.cloned.1.call-start = ((), (), s32[]{:S(2)}) async-start(), calls=%async_computation.2 | async-start | bytes 8847360 | tf_op jit(solution)/shard_map/all_gather | solution.py:116
  62.1 97.9 %all-gather.8.cloned.1.call-start = ((), (), s32[]{:S(2)}) async-start(), calls=%async_computation.3 | async-start | bytes 7864320 | tf_op jit(solution)/shard_map/all_gather | solution.py:119
  160.0 1.2 copy-start.7
  161.2 25.3 %copy-start.6 = (bf16[288,1536]{1,0:T(8,128)(2,1)S(1)}, bf16[288,1536]{1,0:T(8,128)(2,1)}, u32[]{:S(2)}) copy-start(bf16[288,1536]{1,0:T(8,128)(2,1)} %get-tuple-element.11.window_ref) | copy-start | bytes 2654212
  184.9 49.6 %collective-permute-start = (bf16[1024,768]{1,0:T(8,128)(2,1)S(1)}, bf16[1024,768]{1,0:T(8,128)(2,1)S(1)}, u32[]{:S(2)}, u32[]{:S(2)}) collective-permute-start(bf16[1024,768]{1,0:T(8,128)(2,1)S(1)} %shard_map.82), channel_id=1, source_target_pairs={{0,1},{1,0},{2,3},{3,2},{4,5},{5,4},{6,7},{7,6},{8,9},{9,8},{10,11... | collective-permute-start | bytes 4718600 | tf_op jit(solution)/shard_map/ppermute | solution.py:136
  186.5 24.4 %copy-start.5 = (bf16[288,1536]{1,0:T(8,128)(2,1)S(1)}, bf16[288,1536]{1,0:T(8,128)(2,1)}, u32[]{:S(2)}) copy-start(bf16[288,1536]{1,0:T(8,128)(2,1)} %get-tuple-element.12.window_ref) | copy-start | bytes 2654212
  210.2 75.4 %collective-permute-start.2 = (bf16[1024,768]{1,0:T(8,128)(2,1)S(1)}, bf16[1024,768]{1,0:T(8,128)(2,1)S(1)}, u32[]{:S(2)}, u32[]{:S(2)}) collective-permute-start(bf16[1024,768]{1,0:T(8,128)(2,1)S(1)} %shard_map.84), channel_id=1, source_target_pairs={{0,1},{1,0},{2,3},{3,2},{4,5},{5,4},{6,7},{7,6},{8,9},{9,8},{10,11... | collective-permute-start | bytes 4718600 | tf_op jit(solution)/shard_map/ppermute | solution.py:136
  234.6 2.1 copy-start.4
  235.0 50.7 %collective-permute-start.1 = (bf16[1024,768]{1,0:T(8,128)(2,1)S(1)}, bf16[1024,768]{1,0:T(8,128)(2,1)S(1)}, u32[]{:S(2)}, u32[]{:S(2)}) collective-permute-start(bf16[1024,768]{1,0:T(8,128)(2,1)S(1)} %add_convert_fusion.3), channel_id=1, source_target_pairs={{0,2},{1,3},{2,4},{3,5},{4,6},{5,7},{6,0},{7,1},{8,10},{9,11},{10,... | collective-permute-start | bytes 4718600 | tf_op jit(solution)/shard_map/ppermute | solution.py:139
  236.7 25.3 %copy-start.3 = (bf16[288,1536]{1,0:T(8,128)(2,1)S(1)}, bf16[288,1536]{1,0:T(8,128)(2,1)}, u32[]{:S(2)}) copy-start(bf16[288,1536]{1,0:T(8,128)(2,1)} %get-tuple-element.10.window_ref) | copy-start | bytes 2654212
  260.5 75.5 %collective-permute-start.4 = (bf16[1024,768]{1,0:T(8,128)(2,1)S(1)}, bf16[1024,768]{1,0:T(8,128)(2,1)S(1)}, u32[]{:S(2)}, u32[]{:S(2)}) collective-permute-start(bf16[1024,768]{1,0:T(8,128)(2,1)S(1)} %shard_map.86), channel_id=1, source_target_pairs={{0,1},{1,0},{2,3},{3,2},{4,5},{5,4},{6,7},{7,6},{8,9},{9,8},{10,11... | collective-permute-start | bytes 4718600 | tf_op jit(solution)/shard_map/ppermute | solution.py:136
  285.6 2.2 copy-start.2
  286.2 49.7 %collective-permute-start.3 = (bf16[1024,768]{1,0:T(8,128)(2,1)S(1)}, bf16[1024,768]{1,0:T(8,128)(2,1)S(1)}, u32[]{:S(2)}, u32[]{:S(2)}) collective-permute-start(bf16[1024,768]{1,0:T(8,128)(2,1)S(1)} %add_convert_fusion.2), channel_id=1, source_target_pairs={{0,2},{1,3},{2,4},{3,5},{4,6},{5,7},{6,0},{7,1},{8,10},{9,11},{10,... | collective-permute-start | bytes 4718600 | tf_op jit(solution)/shard_map/ppermute | solution.py:139
  287.8 24.4 %copy-start.1 = (bf16[288,1536]{1,0:T(8,128)(2,1)S(1)}, bf16[288,1536]{1,0:T(8,128)(2,1)}, u32[]{:S(2)}) copy-start(bf16[288,1536]{1,0:T(8,128)(2,1)} %get-tuple-element.8.window_ref) | copy-start | bytes 2654212
  311.6 51.7 %collective-permute-start.6 = (bf16[1024,768]{1,0:T(8,128)(2,1)S(1)}, bf16[1024,768]{1,0:T(8,128)(2,1)S(1)}, u32[]{:S(2)}, u32[]{:S(2)}) collective-permute-start(bf16[1024,768]{1,0:T(8,128)(2,1)S(1)} %shard_map.88), channel_id=1, source_target_pairs={{0,1},{1,0},{2,3},{3,2},{4,5},{5,4},{6,7},{7,6},{8,9},{9,8},{10,11... | collective-permute-start | bytes 4718600 | tf_op jit(solution)/shard_map/ppermute | solution.py:136
  335.9 2.4 copy-start.9
  335.9 2.4 copy-start.10
  336.5 37.0 %collective-permute-start.5 = (bf16[1024,768]{1,0:T(8,128)(2,1)S(1)}, bf16[1024,768]{1,0:T(8,128)(2,1)}, u32[]{:S(2)}, u32[]{:S(2)}) collective-permute-start(bf16[1024,768]{1,0:T(8,128)(2,1)S(1)} %add_convert_fusion.1), channel_id=1, source_target_pairs={{0,2},{1,3},{2,4},{3,5},{4,6},{5,7},{6,0},{7,1},{8,10},{9,11},{10,... | collective-permute-start | bytes 4718600 | tf_op jit(solution)/shard_map/ppermute | solution.py:139
  338.4 35.1 %copy-start.12 = (f32[1024]{0:T(1024)S(1)}, f32[1024]{0:T(1024)}, u32[]{:S(2)}) copy-start(f32[1024]{0:T(1024)} %param.13) | copy-start | bytes 12292
  362.1 1.1 copy-start.8
  363.2 1.2 copy-start.11
Sparse Core Ops, SparseCore 0:
  9.5 48.6 all-gather.3
  62.2 49.7 all-gather.5
  113.6 46.3 all-gather.7
